TPU v7x, 32 devices: a whole 2x2x4 slice. The times are simulated.
32 devices in a mesh: groups: 2 (over y), rows: 4 (over z), cols: 2 (over x), sub: 2 (over core).
Axes of the slice: x: 2, y: 2, z: 4, core: 2. Of those that a mesh axis runs over, the one named last changes fastest.
Arguments:
- library: bfloat16 [81920, 1024], P(('groups', 'rows', 'cols', 'sub')), parts along dimension 0, as said below
- pick_order: int32 [512], P('groups'), parts along dimension 0, may hold values from 0 to 40959, as said below
Outputs:
- centered: bfloat16 [4, 128, 40960], P('groups', ('rows', 'cols', 'sub')), parts along dimension 0
There are 2 independent parts, one for each index of `groups`. A program takes and returns all parts, laid end to end along the dimension named above; each array names one. Nothing has to cross between parts.
Inputs may be any that keep to these rules, and one draw needn't show every extreme that they name: `library`: every entry is at least 0.02. `pick_order`: the 256 picks are distinct library rows.
All inputs are finite; a program needn't handle non-finite values.
Results may differ from a plain program's by a relative error of at most 0.0063.
Values may be sent and summed in bfloat16 or wider, within the bound.
A program may use at most 64 MiB of HBM per device.

v0:
```python
import jax
import jax.numpy as jnp
from jax import lax
from jax.sharding import PartitionSpec as P

BLOCK = 128
BLOCKS = 2


nugget = 0.1


def tanimoto(products, left_sq, right_sq):
    return products / (left_sq[:, None] + right_sq[None, :] - products)


def pick_table(library, local_picks, owned_mask):
    clipped = jnp.clip(local_picks, 0, library.shape[0] - 1)
    taken = jnp.take(library, clipped, axis=0).astype(jnp.float32)
    return taken * owned_mask[:, None]


def factor_table(factor_panel, local_picks, owned_mask):
    clipped = jnp.clip(local_picks, 0, factor_panel.shape[1] - 1)
    taken = jnp.take(factor_panel, clipped, axis=1)
    return jnp.transpose(taken) * owned_mask[:, None]


def regroup(block_panel):
    block_count, local_rows = block_panel.shape
    devices_all = lax.axis_size(("rows", "cols", "sub"))
    shaped = block_panel.reshape(devices_all, block_count // devices_all, 1, local_rows)
    moved = lax.all_to_all(shaped, ("rows", "cols", "sub"), split_axis=0, concat_axis=2, tiled=True)
    return moved


def center_rows(moved, owned_count):
    values = moved.reshape(owned_count, -1).astype(jnp.float32)
    column_mean = jnp.mean(values, axis=1, keepdims=True)
    return (values - column_mean).astype(jnp.bfloat16)


def local(library, pick_order):
    local_rows = library.shape[0]
    owned_count = BLOCK // lax.axis_size(("rows", "cols", "sub"))
    first_row = lax.axis_index(("rows", "cols", "sub")) * local_rows
    row_ids = first_row + jnp.arange(local_rows, dtype=jnp.int32)
    squares = jnp.sum(jnp.square(library.astype(jnp.float32)), axis=1)
    local_all = pick_order - first_row
    owned_all = ((local_all >= 0) & (local_all < local_rows)).astype(jnp.float32)
    identity = jnp.eye(BLOCK, dtype=jnp.float32)
    factor_panel = None
    prior_rows = None
    results = []
    for block_id in range(BLOCKS):
        lower_end = block_id * BLOCK
        chosen = pick_order[lower_end : lower_end + BLOCK]
        local_picks = local_all[lower_end : lower_end + BLOCK]
        owned_mask = owned_all[lower_end : lower_end + BLOCK]
        if block_id == 0:
            pick_values = lax.psum(
                pick_table(library, local_picks, owned_mask), ("rows", "cols", "sub")
            )
        else:
            pick_values = lax.psum(
                pick_table(library, local_picks, owned_mask), ("rows", "cols", "sub")
            )
            prior_rows = lax.psum(
                factor_table(factor_panel, local_picks, owned_mask), ("rows", "cols", "sub")
            )
        pick_rows = pick_values.astype(jnp.bfloat16)
        pick_squares = jnp.sum(jnp.square(pick_rows.astype(jnp.float32)), axis=1)
        products = jnp.einsum("sf,nf->sn", pick_rows, library, preferred_element_type=jnp.float32)
        marker = (chosen[:, None] == row_ids[None, :]).astype(jnp.float32)
        residual = tanimoto(products, pick_squares, squares) + nugget * marker
        pick_products = jnp.dot(pick_rows, pick_rows.T, preferred_element_type=jnp.float32)
        pivot_block = tanimoto(pick_products, pick_squares, pick_squares) + nugget * identity
        if block_id > 0:
            residual = residual - jnp.dot(prior_rows, factor_panel, precision=lax.Precision.HIGHEST)
            pivot_block = pivot_block - jnp.dot(
                prior_rows, prior_rows.T, precision=lax.Precision.HIGHEST
            )
        cholesky_low = jnp.linalg.cholesky(pivot_block)
        inverse = lax.linalg.triangular_solve(cholesky_low, identity, left_side=True, lower=True)
        new_panel = jnp.dot(inverse, residual, precision=lax.Precision.HIGHEST)
        factor_panel = (
            new_panel if block_id == 0 else jnp.concatenate([factor_panel, new_panel], axis=0)
        )
        moved = regroup(new_panel.astype(jnp.bfloat16))
        results.append(center_rows(moved, owned_count))
    return jnp.stack(results, axis=0)


def solution(mesh):
    placed = (P(("groups", "rows", "cols", "sub"), None), P("groups"))
    return jax.shard_map(
        local,
        mesh=mesh,
        in_specs=placed,
        out_specs=P("groups", ("rows", "cols", "sub"), None),
        check_vma=False,
    )
```

profile of v0, /device:TPU:0, one launch (start us, length us, event | category | flops | bytes accessed | tf_op | source)
XLA Modules:
  0.0 271.7 jit_solution(11284344431556010509)
XLA Ops:
  6.5 0.7 and_convert_fusion
  7.3 4.2 %gather_fusion.2 = bf16[128,1024]{1,0:T(8,128)(2,1)S(1)} fusion(bf16[2560,1024]{1,0:T(8,128)(2,1)} %param.7, s32[1024]{0:T(1024)S(1)} %pad_clamp_fusion), kind=kCustom, calls=%fused_computation.1.clone | custom fusion | bytes 524800 | tf_op jit(solution)/shard_map/jit(_take)/gather | solution.py:19
  11.5 4.2 %gather_fusion.1 = bf16[128,1024]{1,0:T(8,128)(2,1)S(1)} fusion(bf16[2560,1024]{1,0:T(8,128)(2,1)} %param.7, s32[1024]{0:T(1024)S(1)} %pad_clamp_fusion.1), kind=kCustom, calls=%fused_computation.clone | custom fusion | bytes 524800 | tf_op jit(solution)/shard_map/jit(_take)/gather | solution.py:19
  15.9 75.0 %all-reduce.5 = (bf16[128,1024]{1,0:T(8,128)(2,1)S(1)}, bf16[128,1024]{1,0:T(8,128)(2,1)S(1)}) all-reduce(f32[128,1024]{1,0:T(8,128)S(1)} %get-tuple-element.23, f32[128,1024]{1,0:T(8,128)S(1)} %get-tuple-element.22), channel_id=1, replica_groups=mesh['groups'=2,'rows'=4,'cols'=2,'sub'=2] {'rows','cols','sub'}, use_global_device_ids=true, to_apply=%region_0.2 | all-reduce | flops 262144 | bytes 1572864 | tf_op jit(solution)/shard_map/psum | solution.py:61
  91.1 4.5 %fusion.40 = f32[128,2560]{1,0:T(8,128)S(1)} fusion(bf16[128,1024]{1,0:T(8,128)(2,1)S(1)} %get-tuple-element.6, bf16[2560,1024]{1,0:T(8,128)(2,1)} %param.7), kind=kOutput, calls=%fused_computation.83 | convolution fusion | flops 671088640 | bytes 6815744 | tf_op jit(solution)/shard_map/sf,nf->sn/dot_general | solution.py:73
  95.6 1.1 multiply_reduce_fusion
  97.5 11.7 %cholesky.44 = f32[128,128]{1,0:T(8,128)S(1)} custom-call(f32[128,128]{1,0:T(8,128)S(1)} %fusion.23), custom_call_target="Cholesky" | custom-call | tf_op jit(solution)/shard_map/jit(cholesky)/cholesky | solution.py:83
  109.9 0.7 fusion.18
  110.6 9.8 %custom-call.6 = f32[1,128,128]{1,2,0:T(8,128)S(1)} custom-call(f32[1,128,128]{2,1,0:T(8,128)S(1)} %fusion.18), custom_call_target="InvertDiagBlocksLowerTriangular" | custom-call | tf_op jit(solution)/shard_map/triangular_solve/custom-call.0 | solution.py:84
  120.7 1.6 fusion.2
  123.3 0.7 select_multiply_fusion
  124.1 0.9 convert_bitcast_fusion
  125.0 3.8 %all-to-all-start = ((bf16[16,8,1,2560]{3,1,2,0:T(8,128)(2,1)}), bf16[16,8,1,2560]{3,1,2,0:T(8,128)(2,1)S(1)}, u32[]{:S(2)}, u32[]{:S(2)}) async-start(bf16[16,8,1,2560]{3,1,2,0:T(8,128)(2,1)} %convert_bitcast_fusion), calls=%async_computation | async-start | bytes 1310720 | tf_op jit(solution)/shard_map/all_to_all | solution.py:33
  128.8 0.8 fusion.39
  129.7 4.4 %fusion.38 = f32[128,2560]{1,0:T(8,128)S(1)} fusion(bf16[128,1024]{1,0:T(8,128)(2,1)S(1)} %get-tuple-element.8, bf16[2560,1024]{1,0:T(8,128)(2,1)} %param.7), kind=kOutput, calls=%fused_computation.81 | convolution fusion | flops 671088640 | bytes 6815744 | tf_op jit(solution)/shard_map/sf,nf->sn/dot_general | solution.py:73
  134.2 76.9 %all-reduce.4.cloned.1.call-done = f32[128,128]{1,0:T(8,128)} async-done(((f32[128,128]{1,0:T(8,128)}), f32[128,128]{1,0:T(8,128)}) %all-reduce.4.cloned.1.call-update) | async-done | bytes 65552 | tf_op jit(solution)/shard_map/psum | solution.py:68
  211.1 1.2 convolution_subtract_fusion.1
  212.4 11.7 %cholesky.55 = f32[128,128]{1,0:T(8,128)S(1)} custom-call(f32[128,128]{1,0:T(8,128)S(1)} %fusion.21), custom_call_target="Cholesky" | custom-call | tf_op jit(solution)/shard_map/jit(cholesky)/cholesky | solution.py:83
  225.4 9.8 %custom-call.7 = f32[1,128,128]{1,2,0:T(8,128)S(1)} custom-call(f32[1,128,128]{2,1,0:T(8,128)S(1)} %fusion.19), custom_call_target="InvertDiagBlocksLowerTriangular" | custom-call | tf_op jit(solution)/shard_map/triangular_solve/custom-call.0 | solution.py:84
  235.5 2.4 convolution_subtract_fusion
  237.9 2.1 fusion
  240.0 6.3 %all-to-all-start.1 = ((bf16[16,8,1,2560]{3,1,2,0:T(8,128)(2,1)}), bf16[16,8,1,2560]{3,1,2,0:T(8,128)(2,1)S(1)}, u32[]{:S(2)}, u32[]{:S(2)}) async-start(bf16[16,8,1,2560]{3,1,2,0:T(8,128)(2,1)} %fusion), calls=%async_computation.1 | async-start | bytes 1310720 | tf_op jit(solution)/shard_map/all_to_all | solution.py:33
  247.1 15.9 %all-to-all-done.1 = bf16[16,8,1,2560]{3,1,2,0:T(8,128)(2,1)S(1)} async-done(((bf16[16,8,1,2560]{3,1,2,0:T(8,128)(2,1)}), bf16[16,8,1,2560]{3,1,2,0:T(8,128)(2,1)S(1)}, u32[]{:S(2)}, u32[]{:S(2)}) %all-to-all-start.1) | async-done | bytes 655392 | tf_op jit(solution)/shard_map/all_to_all | solution.py:33
  263.7 1.2 pad_maximum_fusion
  (40 shorter events, 6.6 us)
Async XLA Ops:
  6.5 204.5 %all-reduce.4.cloned.1.call-start = ((), (), s32[]{:S(2)}) async-start(), calls=%async_computation.2 | async-start | bytes 131072 | tf_op jit(solution)/shard_map/psum | solution.py:68
  91.1 4.5 %copy-start = (bf16[2560,1024]{1,0:T(8,128)(2,1)S(1)}, bf16[2560,1024]{1,0:T(8,128)(2,1)}, u32[]{:S(2)}) copy-start(bf16[2560,1024]{1,0:T(8,128)(2,1)} %param.7) | copy-start | bytes 15728644
  95.6 1.1 copy-start.2
  96.7 25.6 %copy-start.1 = (f32[2560]{0:T(1024)}, f32[2560]{0:T(1024)S(1)}, u32[]{:S(2)}) copy-start(f32[2560]{0:T(1024)S(1)} %multiply_reduce_fusion) | copy-start | bytes 30724
  125.0 115.0 %all-to-all-start = ((bf16[16,8,1,2560]{3,1,2,0:T(8,128)(2,1)}), bf16[16,8,1,2560]{3,1,2,0:T(8,128)(2,1)S(1)}, u32[]{:S(2)}, u32[]{:S(2)}) async-start(bf16[16,8,1,2560]{3,1,2,0:T(8,128)(2,1)} %convert_bitcast_fusion), calls=%async_computation | async-start | bytes 1310720 | tf_op jit(solution)/shard_map/all_to_all | solution.py:33
  240.0 22.9 %all-to-all-start.1 = ((bf16[16,8,1,2560]{3,1,2,0:T(8,128)(2,1)}), bf16[16,8,1,2560]{3,1,2,0:T(8,128)(2,1)S(1)}, u32[]{:S(2)}, u32[]{:S(2)}) async-start(bf16[16,8,1,2560]{3,1,2,0:T(8,128)(2,1)} %fusion), calls=%async_computation.1 | async-start | bytes 1310720 | tf_op jit(solution)/shard_map/all_to_all | solution.py:33
Sparse Core Ops, SparseCore 0:
  124.2 86.7 all-reduce.3
where the time goes:
time: 272 us
  waiting for transfers between devices  92.8 us (34%)
  blocking collectives  75 us (28%)
  other arithmetic  52.3 us (19%)
  matrix products  17.7 us (7%)
  between operations  13.7 us (5%)
  starting transfers between devices  10.1 us (4%)
  local copies, waits for them, and re-layouts  10.1 us (4%)
    psum x1, waiting for transfers between devices, local(): lax.psum(factor_table(factor_panel, local_picks, owned_mask), ('rows', 'c...  76.9 us
    psum x1, blocking collectives, local(): lax.psum(pick_table(library, local_picks, owned_mask), ('rows', 'cols', '...  75 us
    another operation x6, other arithmetic, local(): cholesky_low = jnp.linalg.cholesky(pivot_block)  24.8 us
    another operation x4, other arithmetic, local(): lax.linalg.triangular_solve(cholesky_low, identity, left_side=True, lower...  20.9 us
    all_to_all x2, waiting for transfers between devices, regroup(): lax.all_to_all(shaped, ('rows', 'cols', 'sub'), split_axis=0, concat_axis...  15.9 us
    all_to_all x2, starting transfers between devices, regroup(): lax.all_to_all(shaped, ('rows', 'cols', 'sub'), split_axis=0, concat_axis...  10.1 us
    dot_general x2, matrix products, local(): jnp.einsum('sf,nf->sn', pick_rows, library, preferred_element_type=jnp.fl...  8.83 us
    gather x2, local copies, waits for them, and re-layouts, pick_table(): taken = jnp.take(library, clipped, axis=0).astype(jnp.float32)  8.41 us
  transfers between devices with their start and end apart: 3, of which 2 were waited for; matrix products, arithmetic and copies ran while one was open for 13% of the time, Pallas kernels for 0%

commit v1 on v0

v1 whole, which is shorter than its diff:
```python
import functools

import jax
import jax.numpy as jnp
from jax import lax
from jax.experimental import pallas as pl
from jax.experimental.pallas import tpu as pltpu
from jax.sharding import PartitionSpec as P

BLOCK = 128
BLOCKS = 2
GROUP = 16
SPREAD = ("rows", "cols", "sub")
MESH = pl.DeviceIdType.MESH
HIGHEST = lax.Precision.HIGHEST

nugget = 0.1


def tanimoto(products, left_sq, right_sq):
    return products / (left_sq[:, None] + right_sq[None, :] - products)


def pick_table(library, local_picks, owned_mask):
    clipped = jnp.clip(local_picks, 0, library.shape[0] - 1)
    taken = jnp.take(library, clipped, axis=0).astype(jnp.float32)
    return taken * owned_mask[:, None]


def regroup(block_panel):
    block_count, local_rows = block_panel.shape
    devices_all = lax.axis_size(SPREAD)
    shaped = block_panel.reshape(devices_all, block_count // devices_all, 1, local_rows)
    moved = lax.all_to_all(shaped, SPREAD, split_axis=0, concat_axis=2, tiled=True)
    return moved


def center_rows(moved, owned_count):
    values = moved.reshape(owned_count, -1).astype(jnp.float32)
    column_mean = jnp.mean(values, axis=1, keepdims=True)
    return (values - column_mean).astype(jnp.bfloat16)


def exchange_stages(sizes):
    stages = []
    for axis in ("sub", "cols", "rows"):
        bit = 1
        while bit < sizes[axis]:
            stages.append((axis, bit))
            bit *= 2
    return stages


def flipped(axis, bit):
    index = lax.axis_index(axis)
    high = lax.rem(index // bit, 2)
    return index + bit - 2 * bit * high, high


def gather_kernel(stages, local_ref, library_ref, out_ref, table, *rest):
    count = len(stages)
    landing = rest[:count]
    send_sem, recv_sem = rest[count:]
    barrier = pltpu.get_barrier_semaphore()
    partners = []
    for axis, bit in stages:
        other, high = flipped(axis, bit)
        partners.append((axis, other, high))
        pl.semaphore_signal(barrier, inc=1, device_id={axis: other}, device_id_type=MESH)
    picks, features = table.shape
    rows = library_ref.shape[0]
    hot = (local_ref[...] == lax.broadcasted_iota(jnp.int32, (picks, rows), 1)).astype(jnp.bfloat16)
    tile = 256
    for start in range(0, features, tile):
        table[:, start : start + tile] = jnp.dot(
            hot, library_ref[:, start : start + tile], preferred_element_type=jnp.float32
        ).astype(jnp.bfloat16)
    pl.semaphore_wait(barrier, count)
    base = 0
    size = picks
    bases = []
    for step, (axis, other, high) in enumerate(partners):
        size //= 2
        keep = pl.multiple_of(base + high * size, 16)
        give = pl.multiple_of(base + (1 - high) * size, 16)
        copy = pltpu.make_async_remote_copy(
            src_ref=table.at[pl.ds(give, size)],
            dst_ref=landing[step],
            send_sem=send_sem.at[step],
            recv_sem=recv_sem.at[step],
            device_id={axis: other},
            device_id_type=MESH,
        )
        copy.start()
        copy.wait()
        total = table[pl.ds(keep, size), :] + landing[step][...]
        if step < count - 1:
            table[pl.ds(keep, size), :] = total
        else:
            out_ref[pl.ds(keep, size), :] = total
        base = keep
        bases.append(keep)
    for step in reversed(range(count)):
        axis, other, high = partners[step]
        held = pl.multiple_of(bases[step], 16)
        copy = pltpu.make_async_remote_copy(
            src_ref=out_ref.at[pl.ds(held, size)],
            dst_ref=out_ref.at[pl.ds(held, size)],
            send_sem=send_sem.at[count + step],
            recv_sem=recv_sem.at[count + step],
            device_id={axis: other},
            device_id_type=MESH,
        )
        copy.start()
        copy.wait()
        size *= 2


def gather_picks(library, local_all):
    picks = local_all.shape[0]
    features = library.shape[1]
    sizes = {axis: lax.axis_size(axis) for axis in SPREAD}
    stages = exchange_stages(sizes)
    scratch = [pltpu.VMEM((picks, features), jnp.bfloat16)]
    size = picks
    for _ in stages:
        size //= 2
        scratch.append(pltpu.VMEM((size, features), jnp.bfloat16))
    scratch += [pltpu.SemaphoreType.DMA((2 * len(stages),))] * 2
    return pl.pallas_call(
        functools.partial(gather_kernel, stages),
        out_shape=jax.ShapeDtypeStruct((picks, features), jnp.bfloat16),
        in_specs=[pl.BlockSpec(memory_space=pltpu.VMEM)] * 2,
        out_specs=pl.BlockSpec(memory_space=pltpu.VMEM),
        scratch_shapes=scratch,
        compiler_params=pltpu.CompilerParams(
            collective_id=0, has_side_effects=True, vmem_limit_bytes=40 * 2**20
        ),
        name="gather_picks",
    )(local_all[:, None], library)


def eliminate(left, right):
    size = left.shape[0]
    sub = lax.broadcasted_iota(jnp.int32, (GROUP, size), 0)
    for start in range(0, size, GROUP):
        stop = start + GROUP
        top = left[start:stop, :]
        low = right[start:stop, :]
        columns = [
            jnp.broadcast_to(top[:, start + j : start + j + 1], (GROUP, size)) for j in range(GROUP)
        ]
        pivots = jnp.ones((GROUP, size), jnp.float32)
        for j in range(GROUP):
            pivot = columns[j][j : j + 1, :]
            pivots = jnp.where(sub == j, pivot, pivots)
            factor = jnp.where(sub > j, columns[j] * (1.0 / pivot), 0.0)
            top = top - factor * top[j : j + 1, :]
            low = low - factor * low[j : j + 1, :]
            for k in range(j + 1, GROUP):
                columns[k] = columns[k] - factor * columns[k][j : j + 1, :]
        scale = lax.rsqrt(pivots)
        top = top * scale
        low = low * scale
        right[start:stop, :] = low
        if stop < size:
            side = jnp.transpose(top)[stop:, :]
            both = jnp.concatenate([top, low], axis=1)
            update = jnp.dot(side, both, precision=HIGHEST, preferred_element_type=jnp.float32)
            left[stop:, :] = left[stop:, :] - update[:, :size]
            right[stop:, :] = right[stop:, :] - update[:, size:]


def identity_of(size):
    ones = lax.broadcasted_iota(jnp.int32, (size, size), 0) == lax.broadcasted_iota(
        jnp.int32, (size, size), 1
    )
    return ones.astype(jnp.float32)


def inverse_kernel(first_ref, cross_ref, second_ref, inverse_ref, prior_ref, left):
    size = first_ref.shape[0]
    eye = identity_of(size)
    left[...] = first_ref[...]
    inverse_ref[0] = eye
    eliminate(left, inverse_ref.at[0])
    prior = jnp.dot(
        inverse_ref[0], cross_ref[...], precision=HIGHEST, preferred_element_type=jnp.float32
    )
    prior_t = jnp.transpose(prior)
    prior_ref[...] = prior_t
    left[...] = second_ref[...] - jnp.dot(
        prior_t, prior, precision=HIGHEST, preferred_element_type=jnp.float32
    )
    inverse_ref[1] = eye
    eliminate(left, inverse_ref.at[1])


def inverses(first, cross, second):
    size = first.shape[0]
    vmem = pl.BlockSpec(memory_space=pltpu.VMEM)
    return pl.pallas_call(
        inverse_kernel,
        out_shape=(
            jax.ShapeDtypeStruct((2, size, size), jnp.float32),
            jax.ShapeDtypeStruct((size, size), jnp.float32),
        ),
        in_specs=[vmem] * 3,
        out_specs=(vmem, vmem),
        scratch_shapes=[pltpu.VMEM((size, size), jnp.float32)],
        compiler_params=pltpu.CompilerParams(vmem_limit_bytes=24 * 2**20),
        name="inverses",
    )(first, cross, second)


def local(library, pick_order):
    local_rows = library.shape[0]
    devices = lax.axis_size(SPREAD)
    owned_count = BLOCK // devices
    first_row = lax.axis_index(SPREAD) * local_rows
    row_ids = first_row + jnp.arange(local_rows, dtype=jnp.int32)
    local_all = pick_order - first_row
    if pick_order.shape[0] % (16 * devices) == 0:
        pick_rows = gather_picks(library, local_all)
    else:
        owned_all = ((local_all >= 0) & (local_all < local_rows)).astype(jnp.float32)
        pick_rows = lax.psum(pick_table(library, local_all, owned_all), SPREAD)
        pick_rows = pick_rows.astype(jnp.bfloat16)
    squares = jnp.sum(jnp.square(library.astype(jnp.float32)), axis=1)
    pick_squares = jnp.sum(jnp.square(pick_rows.astype(jnp.float32)), axis=1)
    pick_products = jnp.dot(pick_rows, pick_rows.T, preferred_element_type=jnp.float32)
    pivot = tanimoto(pick_products, pick_squares, pick_squares)
    pivot = pivot + nugget * jnp.eye(pivot.shape[0], dtype=jnp.float32)
    inverse, prior_rows = inverses(
        pivot[:BLOCK, :BLOCK], pivot[:BLOCK, BLOCK:], pivot[BLOCK:, BLOCK:]
    )
    products = jnp.einsum("sf,nf->sn", pick_rows, library, preferred_element_type=jnp.float32)
    marker = (pick_order[:, None] == row_ids[None, :]).astype(jnp.float32)
    kernel = tanimoto(products, pick_squares, squares) + nugget * marker
    first = jnp.dot(inverse[0], kernel[:BLOCK], precision=HIGHEST)
    moved = regroup(first.astype(jnp.bfloat16))
    residual = kernel[BLOCK:] - jnp.dot(prior_rows, first, precision=HIGHEST)
    second = jnp.dot(inverse[1], residual, precision=HIGHEST)
    results = [center_rows(moved, owned_count)]
    results.append(center_rows(regroup(second.astype(jnp.bfloat16)), owned_count))
    return jnp.stack(results, axis=0)


def solution(mesh):
    placed = (P(("groups", "rows", "cols", "sub"), None), P("groups"))
    return jax.shard_map(
        local,
        mesh=mesh,
        in_specs=placed,
        out_specs=P("groups", ("rows", "cols", "sub"), None),
        check_vma=False,
    )
```

time: 272 us -> 96.1 us (0.35)
  blocking collectives: 75 us -> 0 us
  waiting for transfers between devices: 92.8 us -> 28.1 us
  other arithmetic: 52.3 us -> 7.97 us
  Pallas kernels: 0 us -> 38 us
  between operations: 13.7 us -> 0.14 us
  matrix products: 17.7 us -> 8.08 us
  local copies, waits for them, and re-layouts: 10.1 us -> 2.93 us
    psum x1 -> x0, waiting for transfers between devices: 76.9 us -> none  [local(): lax.psum(factor_table(factor_panel, local_picks, owned_mask), ('rows', 'c...]
    psum x1 -> x0, blocking collectives: 75 us -> none  [local(): lax.psum(pick_table(library, local_picks, owned_mask), ('rows', 'cols', '...]
    another operation x10 -> x0, other arithmetic: 45.7 us -> none  [the longest x6 24.8 us: local(): cholesky_low = jnp.linalg.cholesky(pivot_block)]
    pallas_call x0 -> x2, Pallas kernels: none -> 38 us  [the longest x1 28.8 us: gather_picks(): pl.pallas_call(functools.partial(gather_kernel, stages), out_shape=jax.Sh...]
    all_to_all x2, waiting for transfers between devices: 15.9 us -> 28.1 us  [regroup(): lax.all_to_all(shaped, SPREAD, split_axis=0, concat_axis=2, tiled=True)]
    gather x3 -> x0, local copies, waits for them, and re-layouts: 9.06 us -> none  [the longest x2 8.41 us: pick_table(): taken = jnp.take(library, clipped, axis=0).astype(jnp.float32)]
    dot_general x2 -> x1, matrix products: 8.83 us -> 1.8 us  [local(): jnp.einsum('sf,nf->sn', pick_rows, library, preferred_element_type=jnp.fl...]
    unnamed x6, local copies, waits for them, and re-layouts: 0.01 us -> 2.79 us
  transfers between devices with their start and end apart: 3 -> 2, of which waited for: 2 -> 2; matrix products, arithmetic and copies ran while one was open for 13% -> 5% of each run, Pallas kernels for 0% -> 0%
where the time goes in v1:
time: 96.1 us; the launch traced here: 95.7 us
  Pallas kernels  38 us (40%)
  waiting for transfers between devices  28.1 us (29%)
  starting transfers between devices  10.5 us (11%)
  matrix products  8.08 us (8%)
  other arithmetic  7.97 us (8%)
  local copies, waits for them, and re-layouts  2.93 us (3%)
    pallas_call x1, Pallas kernels, gather_picks(): pl.pallas_call(functools.partial(gather_kernel, stages), out_shape=jax.Sh...  28.8 us
    all_to_all x2, waiting for transfers between devices, regroup(): lax.all_to_all(shaped, SPREAD, split_axis=0, concat_axis=2, tiled=True)  28.1 us
    all_to_all x2, starting transfers between devices, regroup(): lax.all_to_all(shaped, SPREAD, split_axis=0, concat_axis=2, tiled=True)  10.5 us
    pallas_call x1, Pallas kernels, inverses(): pl.pallas_call(inverse_kernel, out_shape=(jax.ShapeDtypeStruct((2, size,...  9.22 us
    reduce_sum x1, other arithmetic, local(): squares = jnp.sum(jnp.square(library.astype(jnp.float32)), axis=1)  3.58 us
    unnamed x6, local copies, waits for them, and re-layouts  2.79 us
    dot_general x1, matrix products, local(): residual = kernel[BLOCK:] - jnp.dot(prior_rows, first, precision=HIGHEST)  2.57 us
    dot_general x1, matrix products, local(): second = jnp.dot(inverse[1], residual, precision=HIGHEST)  2.09 us
  transfers between devices with their start and end apart: 2, of which 2 were waited for; matrix products, arithmetic and copies ran while one was open for 5% of the time, Pallas kernels for 0%

profile of v1, /device:TPU:0, one launch (start us, length us, event | category | flops | bytes accessed | tf_op | source)
XLA Modules:
  0.0 95.7 jit_solution(3948946011533276308)
XLA Ops:
  0.0 0.7 broadcast_subtract_fusion
  0.7 3.6 %multiply_reduce_fusion = f32[2560]{0:T(1024)S(1)} fusion(bf16[2560,1024]{1,0:T(8,128)(2,1)} %library_ref.1), kind=kLoop, calls=%fused_computation | loop fusion | flops 7861760 | bytes 5253120 | tf_op jit(solution)/shard_map/reduce_sum | solution.py:229
  4.3 0.1 copy.4.local_ref
  4.4 2.5 %copy-done = bf16[2560,1024]{1,0:T(8,128)(2,1)S(1)} copy-done((bf16[2560,1024]{1,0:T(8,128)(2,1)S(1)}, bf16[2560,1024]{1,0:T(8,128)(2,1)}, u32[]{:S(2)}) %copy-start) | copy-done | bytes 5242904
  6.9 28.8 %gather_picks.1 = bf16[256,1024]{1,0:T(8,128)(2,1)S(1)} custom-call(s32[256,1]{1,0:T(8,128)S(1)} %copy.4.local_ref, bf16[2560,1024]{1,0:T(8,128)(2,1)S(1)} %copy-done), custom_call_target="tpu_custom_call" | custom-call | tf_op jit(solution)/shard_map/gather_picks/pallas_call | solution.py:130
  35.7 0.2 multiply_reduce_fusion.1
  35.9 0.3 fusion.4
  36.3 0.3 copy-done.2
  36.6 1.8 %fusion.1 = f32[256,2560]{1,0:T(8,128)S(1)} fusion(s32[2560]{0:T(1024)S(1)} %iota_add_fusion, f32[2560]{0:T(1024)S(1)} %multiply_reduce_fusion, f32[256]{0:T(256)S(1)} %multiply_reduce_fusion.1, s32[256]{0:T(256)S(1)} %copy-done.2, bf16[256,1024]{1,0:T(8,128)(2,1)S(1)} %gather_picks.1, bf16[2560,1024]{1,0:T(8,128)(2,1)S(1)} %copy-done), kind=kOutput, calls=%fused_computation.5 | convolution fusion | flops 1346109440 | bytes 8411136 | tf_op jit(solution)/shard_map/sf,nf->sn/dot_general | solution.py:237
  38.4 9.2 %inverses.1 = (f32[2,128,128]{2,1,0:T(8,128)S(1)}, f32[128,128]{1,0:T(8,128)S(1)}) custom-call(f32[128,128]{1,0:T(8,128)S(1)} %get-tuple-element.11.first_ref, f32[128,128]{1,0:T(8,128)S(1)} %get-tuple-element.10.cross_ref, f32[128,128]{1,0:T(8,128)S(1)} %get-tuple-element.9.second_ref), custom_call_target="tpu_custom_call" | custom-call | tf_op jit(solution)/shard_map/inverses/pallas_call | solution.py:202
  47.6 1.3 %fusion.2 = f32[128,2560]{1,0:T(8,128)S(1)} fusion(f32[256,2560]{1,0:T(8,128)S(1)} %fusion.1, f32[2,128,128]{2,1,0:T(8,128)S(1)} %get-tuple-element.7), kind=kOutput, calls=%fused_computation.6 | convolution fusion | flops 503316480 | bytes 2686976 | tf_op jit(solution)/shard_map/dot_general | solution.py:240
  48.9 0.9 convert_bitcast_fusion
  49.8 5.7 %all-to-all-start = ((bf16[16,8,1,2560]{3,1,2,0:T(8,128)(2,1)}), bf16[16,8,1,2560]{3,1,2,0:T(8,128)(2,1)S(1)}, u32[]{:S(2)}, u32[]{:S(2)}) async-start(bf16[16,8,1,2560]{3,1,2,0:T(8,128)(2,1)} %convert_bitcast_fusion), calls=%async_computation | async-start | bytes 1310720 | tf_op jit(solution)/shard_map/all_to_all | solution.py:34
  55.5 2.6 %convolution_subtract_fusion = f32[128,2560]{1,0:T(8,128)S(1)} fusion(f32[128,128]{1,0:T(8,128)S(1)} %get-tuple-element.8, f32[128,2560]{1,0:T(8,128)S(1)} %fusion.2, f32[256,2560]{1,0:T(8,128)} %copy-done.1), kind=kOutput, calls=%fused_computation.2 | convolution fusion | flops 503644160 | bytes 3997696 | tf_op jit(solution)/shard_map/dot_general | solution.py:242
  58.1 2.1 %fusion = bf16[16,8,1,2560]{3,1,2,0:T(8,128)(2,1)} fusion(f32[128,2560]{1,0:T(8,128)S(1)} %convolution_subtract_fusion, f32[2,128,128]{2,1,0:T(8,128)S(1)} %get-tuple-element.7), kind=kOutput, calls=%fused_computation.4 | convolution fusion | flops 503644160 | bytes 2031616 | tf_op jit(solution)/shard_map/dot_general | solution.py:243
  60.2 11.9 %all-to-all-done = bf16[16,8,1,2560]{3,1,2,0:T(8,128)(2,1)S(1)} async-done(((bf16[16,8,1,2560]{3,1,2,0:T(8,128)(2,1)}), bf16[16,8,1,2560]{3,1,2,0:T(8,128)(2,1)S(1)}, u32[]{:S(2)}, u32[]{:S(2)}) %all-to-all-start) | async-done | bytes 655392 | tf_op jit(solution)/shard_map/all_to_all | solution.py:34
  72.1 4.8 %all-to-all-start.1 = ((bf16[16,8,1,2560]{3,1,2,0:T(8,128)(2,1)}), bf16[16,8,1,2560]{3,1,2,0:T(8,128)(2,1)S(1)}, u32[]{:S(2)}, u32[]{:S(2)}) async-start(bf16[16,8,1,2560]{3,1,2,0:T(8,128)(2,1)} %fusion), calls=%async_computation.1 | async-start | bytes 1310720 | tf_op jit(solution)/shard_map/all_to_all | solution.py:34
  76.9 0.4 convert_reduce_fusion.1
  77.3 16.1 %all-to-all-done.1 = bf16[16,8,1,2560]{3,1,2,0:T(8,128)(2,1)S(1)} async-done(((bf16[16,8,1,2560]{3,1,2,0:T(8,128)(2,1)}), bf16[16,8,1,2560]{3,1,2,0:T(8,128)(2,1)S(1)}, u32[]{:S(2)}, u32[]{:S(2)}) %all-to-all-start.1) | async-done | bytes 655392 | tf_op jit(solution)/shard_map/all_to_all | solution.py:34
  93.5 0.4 convert_reduce_fusion
  93.9 0.1 convert_element_type.103
  94.1 0.1 subtract_convert_fusion
  94.4 0.1 subtract_convert_fusion.1
  94.5 1.2 %pad_maximum_fusion = bf16[2,8,40960]{2,1,0:T(8,128)(2,1)} fusion(bf16[1,8,40960]{2,1,0:T(8,128)(2,1)S(1)} %subtract_convert_fusion, bf16[1,8,40960]{2,1,0:T(8,128)(2,1)S(1)} %subtract_convert_fusion.1), kind=kLoop, calls=%fused_computation.8 | loop fusion | flops 655360 | bytes 2621440 | tf_op jit(solution)/shard_map/stack | solution.py:246
  (9 shorter events, 0.2 us)
Async XLA Ops:
  4.4 2.5 %copy-start = (bf16[2560,1024]{1,0:T(8,128)(2,1)S(1)}, bf16[2560,1024]{1,0:T(8,128)(2,1)}, u32[]{:S(2)}) copy-start(bf16[2560,1024]{1,0:T(8,128)(2,1)} %library_ref.1) | copy-start | bytes 15728644
  35.9 0.7 copy-start.2
  38.4 10.5 %copy-start.1 = (f32[256,2560]{1,0:T(8,128)}, f32[256,2560]{1,0:T(8,128)S(1)}, u32[]{:S(2)}) copy-start(f32[256,2560]{1,0:T(8,128)S(1)} %fusion.1) | copy-start | bytes 7864324
  49.8 22.3 %all-to-all-start = ((bf16[16,8,1,2560]{3,1,2,0:T(8,128)(2,1)}), bf16[16,8,1,2560]{3,1,2,0:T(8,128)(2,1)S(1)}, u32[]{:S(2)}, u32[]{:S(2)}) async-start(bf16[16,8,1,2560]{3,1,2,0:T(8,128)(2,1)} %convert_bitcast_fusion), calls=%async_computation | async-start | bytes 1310720 | tf_op jit(solution)/shard_map/all_to_all | solution.py:34
  72.1 21.4 %all-to-all-start.1 = ((bf16[16,8,1,2560]{3,1,2,0:T(8,128)(2,1)}), bf16[16,8,1,2560]{3,1,2,0:T(8,128)(2,1)S(1)}, u32[]{:S(2)}, u32[]{:S(2)}) async-start(bf16[16,8,1,2560]{3,1,2,0:T(8,128)(2,1)} %fusion), calls=%async_computation.1 | async-start | bytes 1310720 | tf_op jit(solution)/shard_map/all_to_all | solution.py:34

commit v2 on v0

v2 whole, which is shorter than its diff:
```python
import functools

import jax
import jax.numpy as jnp
from jax import lax
from jax.experimental import pallas as pl
from jax.experimental.pallas import tpu as pltpu
from jax.sharding import PartitionSpec as P

BLOCK = 128
BLOCKS = 2
GROUP = 16
SPREAD = ("rows", "cols", "sub")
MESH = pl.DeviceIdType.MESH
HIGHEST = lax.Precision.HIGHEST

nugget = 0.1


def tanimoto(products, left_sq, right_sq):
    return products / (left_sq[:, None] + right_sq[None, :] - products)


def pick_table(library, local_picks, owned_mask):
    clipped = jnp.clip(local_picks, 0, library.shape[0] - 1)
    taken = jnp.take(library, clipped, axis=0).astype(jnp.float32)
    return taken * owned_mask[:, None]


def regroup(block_panel):
    block_count, local_rows = block_panel.shape
    devices_all = lax.axis_size(SPREAD)
    shaped = block_panel.reshape(devices_all, block_count // devices_all, 1, local_rows)
    moved = lax.all_to_all(shaped, SPREAD, split_axis=0, concat_axis=2, tiled=True)
    return moved


def center_rows(moved, owned_count):
    values = moved.reshape(owned_count, -1).astype(jnp.float32)
    column_mean = jnp.mean(values, axis=1, keepdims=True)
    return (values - column_mean).astype(jnp.bfloat16)


def tile_kernel(products, left_sq, right_sq):
    return products / (left_sq + right_sq - products)


def transposed_dot(left, right):
    return lax.dot_general(
        left, right, (((1,), (1,)), ((), ())), preferred_element_type=jnp.float32
    )


def gather_kernel(local_ref, library_ref, kernel_ref, pivot_ref, table, picked, near, far, squares, sub_sem, far_sem):
    sub = lax.axis_index("sub")
    row, col = lax.axis_index("rows"), lax.axis_index("cols")
    row_count, col_count = lax.axis_size("rows"), lax.axis_size("cols")
    chips = row_count * col_count
    me = row * col_count + col
    picks, features = table.shape
    rows = library_ref.shape[0]
    half = BLOCK // 2
    part_rows, part_cols = half // row_count, features // col_count
    other = 1 - sub

    def place(index):
        return {"rows": index // col_count, "cols": lax.rem(index, col_count)}

    barrier = pltpu.get_barrier_semaphore()
    pl.semaphore_signal(barrier, inc=1, device_id={"sub": other}, device_id_type=MESH)
    for k in range(1, chips):
        pl.semaphore_signal(
            barrier, inc=1, device_id=place(lax.rem(me + k, chips)), device_id_type=MESH
        )

    def half_rows(block, which):
        return pl.ds(pl.multiple_of(block * BLOCK + which * half, 16), half)

    def part(ref, block, index):
        first = block * BLOCK + sub * half + (index // col_count) * part_rows
        side = lax.rem(index, col_count) * part_cols
        return ref.at[
            pl.ds(pl.multiple_of(first, 16), part_rows),
            pl.ds(pl.multiple_of(side, 128), part_cols),
        ]

    def sub_copy(source, target, slot):
        return pltpu.make_async_remote_copy(
            src_ref=source,
            dst_ref=target,
            send_sem=sub_sem.at[0, slot],
            recv_sem=sub_sem.at[1, slot],
            device_id={"sub": other},
            device_id_type=MESH,
        )

    def far_copy(source, target, slot, k):
        return pltpu.make_async_remote_copy(
            src_ref=source,
            dst_ref=target,
            send_sem=far_sem.at[0, slot, k - 1],
            recv_sem=far_sem.at[1, slot, k - 1],
            device_id=place(lax.rem(me + k, chips)),
            device_id_type=MESH,
        )

    order = sorted(range(1, chips), key=lambda k: -min(k, chips - k))
    tile = 256
    first = []
    for block in range(BLOCKS):
        span = pl.ds(block * BLOCK, BLOCK)
        hot = local_ref[span, :] == lax.broadcasted_iota(jnp.int32, (BLOCK, rows), 1)
        hot = hot.astype(jnp.float32).astype(jnp.bfloat16)
        for start in range(0, features, tile):
            table[span, start : start + tile] = jnp.dot(
                hot, library_ref[:, start : start + tile], preferred_element_type=jnp.float32
            ).astype(jnp.bfloat16)
        if block == 0:
            pl.semaphore_wait(barrier, chips)
        copy = sub_copy(table.at[half_rows(block, other)], near.at[block], block)
        copy.start()
        first.append(copy)
    second = []
    for block in range(BLOCKS):
        first[block].wait()
        keep = half_rows(block, sub)
        table[keep, :] = table[keep, :] + near[block]
        copies = []
        for k in order:
            copy = far_copy(
                part(table, block, lax.rem(me + k, chips)), far.at[block, k - 1], block, k
            )
            copy.start()
            copies.append(copy)
        second.append(copies)
    ones = jnp.ones((8, features), jnp.bfloat16)
    for start in range(0, rows, tile):
        values = library_ref[start : start + tile, :].astype(jnp.float32)
        values = values * values
        high = values.astype(jnp.bfloat16)
        low = (values - high.astype(jnp.float32)).astype(jnp.bfloat16)
        squares[:, start : start + tile] = transposed_dot(ones, high) + transposed_dot(ones, low)
    third = []
    for block in range(BLOCKS):
        for copy in second[block]:
            copy.wait()
        total = part(table, block, me)[...]
        for k in range(1, chips):
            total = total + far[block, k - 1]
        mine = part(picked, block, me)
        mine[...] = total
        copies = []
        for k in order:
            copy = far_copy(mine, mine, BLOCKS + block, k)
            copy.start()
            copies.append(copy)
        third.append(copies)
    fourth = []
    for block in range(BLOCKS):
        for copy in third[block]:
            copy.wait()
        held = picked.at[half_rows(block, sub)]
        copy = sub_copy(held, held, BLOCKS + block)
        copy.start()
        fourth.append(copy)
    for copy in fourth:
        copy.wait()

    rows_all = picked[...]
    grams = transposed_dot(rows_all, rows_all)
    eye = identity_of(picks)
    across = jnp.sum(grams * eye, axis=0, keepdims=True)
    down = jnp.sum(grams * eye, axis=1, keepdims=True)
    pivot_ref[...] = tile_kernel(grams, down, across) + nugget * eye
    for start in range(0, rows, tile):
        span = slice(start, start + tile)
        products = transposed_dot(rows_all, library_ref[span, :])
        ids = start + lax.broadcasted_iota(jnp.int32, (picks, tile), 1)
        marker = (local_ref[...] == ids).astype(jnp.float32)
        kernel_ref[:, span] = (
            tile_kernel(products, down, squares[0:1, span]) + nugget * marker
        )


def gather_kernels(library, local_all):
    picks = local_all.shape[0]
    rows, features = library.shape
    row_count, col_count = lax.axis_size("rows"), lax.axis_size("cols")
    chips = row_count * col_count
    vmem = pl.BlockSpec(memory_space=pltpu.VMEM)
    half = BLOCK // 2
    return pl.pallas_call(
        gather_kernel,
        out_shape=(
            jax.ShapeDtypeStruct((picks, rows), jnp.float32),
            jax.ShapeDtypeStruct((picks, picks), jnp.float32),
        ),
        in_specs=[vmem] * 2,
        out_specs=(vmem, vmem),
        scratch_shapes=[
            pltpu.VMEM((picks, features), jnp.bfloat16),
            pltpu.VMEM((picks, features), jnp.bfloat16),
            pltpu.VMEM((BLOCKS, half, features), jnp.bfloat16),
            pltpu.VMEM(
                (BLOCKS, chips - 1, half // row_count, features // col_count), jnp.bfloat16
            ),
            pltpu.VMEM((8, rows), jnp.float32),
            pltpu.SemaphoreType.DMA((2, 2 * BLOCKS)),
            pltpu.SemaphoreType.DMA((2, 2 * BLOCKS, chips - 1)),
        ],
        compiler_params=pltpu.CompilerParams(
            collective_id=0, has_side_effects=True, vmem_limit_bytes=40 * 2**20
        ),
        name="gather_kernels",
    )(local_all[:, None], library)


def eliminate(left, right):
    size = left.shape[0]
    sub = lax.broadcasted_iota(jnp.int32, (GROUP, size), 0)
    for start in range(0, size, GROUP):
        stop = start + GROUP
        top = left[start:stop, :]
        low = right[start:stop, :]
        columns = [
            jnp.broadcast_to(top[:, start + j : start + j + 1], (GROUP, size)) for j in range(GROUP)
        ]
        pivots = jnp.ones((GROUP, size), jnp.float32)
        for j in range(GROUP):
            pivot = columns[j][j : j + 1, :]
            pivots = jnp.where(sub == j, pivot, pivots)
            factor = jnp.where(sub > j, columns[j] * (1.0 / pivot), 0.0)
            top = top - factor * top[j : j + 1, :]
            low = low - factor * low[j : j + 1, :]
            for k in range(j + 1, GROUP):
                columns[k] = columns[k] - factor * columns[k][j : j + 1, :]
        scale = lax.rsqrt(pivots)
        top = top * scale
        low = low * scale
        right[start:stop, :] = low
        if stop < size:
            side = jnp.transpose(top)[stop:, :]
            both = jnp.concatenate([top, low], axis=1)
            update = jnp.dot(side, both, precision=HIGHEST, preferred_element_type=jnp.float32)
            left[stop:, :] = left[stop:, :] - update[:, :size]
            right[stop:, :] = right[stop:, :] - update[:, size:]


def identity_of(size):
    ones = lax.broadcasted_iota(jnp.int32, (size, size), 0) == lax.broadcasted_iota(
        jnp.int32, (size, size), 1
    )
    return ones.astype(jnp.float32)


def full_dot(left, right):
    return jnp.dot(left, right, precision=HIGHEST, preferred_element_type=jnp.float32)


def first_kernel(pivot_ref, inverse_ref, prior_ref, second_ref, left):
    left[...] = pivot_ref[:BLOCK, :BLOCK]
    inverse_ref[...] = identity_of(BLOCK)
    eliminate(left, inverse_ref)
    prior = full_dot(inverse_ref[...], pivot_ref[:BLOCK, BLOCK:])
    prior_t = jnp.transpose(prior)
    prior_ref[...] = prior_t
    second_ref[...] = pivot_ref[BLOCK:, BLOCK:] - full_dot(prior_t, prior)


def first_inverse(pivot):
    vmem = pl.BlockSpec(memory_space=pltpu.VMEM)
    square = jax.ShapeDtypeStruct((BLOCK, BLOCK), jnp.float32)
    return pl.pallas_call(
        first_kernel,
        out_shape=(square,) * 3,
        in_specs=[vmem],
        out_specs=(vmem,) * 3,
        scratch_shapes=[pltpu.VMEM((BLOCK, BLOCK), jnp.float32)],
        compiler_params=pltpu.CompilerParams(vmem_limit_bytes=24 * 2**20),
        name="first_inverse",
    )(pivot)


def panel_kernel(inverse_ref, prior_ref, second_ref, kernel_ref, out_ref, left, right, panel, sent, landed, send_sem, recv_sem):
    sizes = [lax.axis_size(axis) for axis in SPREAD]
    row_count, col_count, sub_count = sizes
    devices = row_count * col_count * sub_count
    me = lax.axis_index(SPREAD)
    rows = kernel_ref.shape[1]
    owned = BLOCK // devices

    def place(index):
        return {
            "rows": index // (col_count * sub_count),
            "cols": lax.rem(index // sub_count, col_count),
            "sub": lax.rem(index, sub_count),
        }

    barrier = pltpu.get_barrier_semaphore()
    for k in range(1, devices):
        pl.semaphore_signal(
            barrier, inc=1, device_id=place(lax.rem(me + k, devices)), device_id_type=MESH
        )
    tile = 512
    order = sorted(range(1, devices), key=lambda k: -min(k, devices - k))
    copies = []
    for block in range(BLOCKS):
        if block > 0:
            left[...] = second_ref[...]
            right[...] = identity_of(BLOCK)
            eliminate(left, right)
        for start in range(0, rows, tile):
            span = slice(start, start + tile)
            if block == 0:
                values = full_dot(inverse_ref[...], kernel_ref[:BLOCK, span])
                panel[:, span] = values
            else:
                residual = kernel_ref[BLOCK:, span] - full_dot(prior_ref[...], panel[:, span])
                values = full_dot(right[...], residual)
            sent[block, :, :, span] = values.reshape(devices, owned, tile).astype(jnp.bfloat16)
        if block == 0:
            pl.semaphore_wait(barrier, devices - 1)
        started = []
        for k in order:
            peer = lax.rem(me + k, devices)
            copy = pltpu.make_async_remote_copy(
                src_ref=sent.at[block, peer],
                dst_ref=landed.at[block, k - 1],
                send_sem=send_sem.at[block, k - 1],
                recv_sem=recv_sem.at[block, k - 1],
                device_id=place(peer),
                device_id_type=MESH,
            )
            copy.start()
            started.append(copy)
        copies.append(started)
    for block in range(BLOCKS):
        own = sent[block, me].astype(jnp.float32)
        total = jnp.sum(own, axis=1, keepdims=True)
        for k, copy in zip(order, copies[block]):
            copy.wait()
            total = total + jnp.sum(
                landed[block, k - 1].astype(jnp.float32), axis=1, keepdims=True
            )
        mean = total / (devices * rows)
        for k in range(devices):
            values = sent[block, me] if k == 0 else landed[block, k - 1]
            source = lax.rem(me + devices - k, devices)
            span = pl.ds(pl.multiple_of(source * rows, 128), rows)
            out_ref[block, :, span] = (values.astype(jnp.float32) - mean).astype(jnp.bfloat16)


def centered_panels(inverse, prior_rows, second, kernel):
    rows = kernel.shape[1]
    devices = lax.axis_size(SPREAD)
    owned = BLOCK // devices
    vmem = pl.BlockSpec(memory_space=pltpu.VMEM)
    return pl.pallas_call(
        panel_kernel,
        out_shape=jax.ShapeDtypeStruct((BLOCKS, owned, devices * rows), jnp.bfloat16),
        in_specs=[vmem] * 4,
        out_specs=vmem,
        scratch_shapes=[
            pltpu.VMEM((BLOCK, BLOCK), jnp.float32),
            pltpu.VMEM((BLOCK, BLOCK), jnp.float32),
            pltpu.VMEM((BLOCK, rows), jnp.float32),
            pltpu.VMEM((BLOCKS, devices, owned, rows), jnp.bfloat16),
            pltpu.VMEM((BLOCKS, devices - 1, owned, rows), jnp.bfloat16),
            pltpu.SemaphoreType.DMA((BLOCKS, devices - 1)),
            pltpu.SemaphoreType.DMA((BLOCKS, devices - 1)),
        ],
        compiler_params=pltpu.CompilerParams(
            collective_id=1, has_side_effects=True, vmem_limit_bytes=40 * 2**20
        ),
        name="centered_panels",
    )(inverse, prior_rows, second, kernel)


def whole(pick_rows, library, pick_order, row_ids):
    squares = jnp.sum(jnp.square(library.astype(jnp.float32)), axis=1)
    pick_squares = jnp.sum(jnp.square(pick_rows.astype(jnp.float32)), axis=1)
    pick_products = jnp.dot(pick_rows, pick_rows.T, preferred_element_type=jnp.float32)
    pivot = tanimoto(pick_products, pick_squares, pick_squares)
    pivot = pivot + nugget * jnp.eye(pivot.shape[0], dtype=jnp.float32)
    products = jnp.einsum("sf,nf->sn", pick_rows, library, preferred_element_type=jnp.float32)
    marker = (pick_order[:, None] == row_ids[None, :]).astype(jnp.float32)
    return tanimoto(products, pick_squares, squares) + nugget * marker, pivot


def local(library, pick_order):
    local_rows, features = library.shape
    sizes = {axis: lax.axis_size(axis) for axis in SPREAD}
    devices = lax.axis_size(SPREAD)
    owned_count = BLOCK // devices
    first_row = lax.axis_index(SPREAD) * local_rows
    local_all = pick_order - first_row
    fits = (
        sizes["sub"] == 2
        and BLOCK % (2 * sizes["rows"] * 16) == 0
        and features % (sizes["cols"] * 128) == 0
        and BLOCK % (devices * 8) == 0
        and local_rows % 512 == 0
        and features % 256 == 0
    )
    if fits:
        kernel, pivot = gather_kernels(library, local_all)
        inverse, prior_rows, second = first_inverse(pivot)
        return centered_panels(inverse, prior_rows, second, kernel)
    owned_all = ((local_all >= 0) & (local_all < local_rows)).astype(jnp.float32)
    pick_rows = lax.psum(pick_table(library, local_all, owned_all), SPREAD)
    row_ids = first_row + jnp.arange(local_rows, dtype=jnp.int32)
    kernel, pivot = whole(pick_rows.astype(jnp.bfloat16), library, pick_order, row_ids)
    inverse, prior_rows, second = first_inverse(pivot)
    panel = jnp.dot(inverse, kernel[:BLOCK], precision=HIGHEST)
    moved = regroup(panel.astype(jnp.bfloat16))
    lower = jnp.linalg.cholesky(second)
    identity = jnp.eye(BLOCK, dtype=jnp.float32)
    inverse = lax.linalg.triangular_solve(lower, identity, left_side=True, lower=True)
    residual = kernel[BLOCK:] - jnp.dot(prior_rows, panel, precision=HIGHEST)
    panel = jnp.dot(inverse, residual, precision=HIGHEST)
    results = [center_rows(moved, owned_count)]
    results.append(center_rows(regroup(panel.astype(jnp.bfloat16)), owned_count))
    return jnp.stack(results, axis=0)


def solution(mesh):
    placed = (P(("groups", "rows", "cols", "sub"), None), P("groups"))
    return jax.shard_map(
        local,
        mesh=mesh,
        in_specs=placed,
        out_specs=P("groups", ("rows", "cols", "sub"), None),
        check_vma=False,
    )
```

time: 272 us -> 66.6 us (0.24)
  waiting for transfers between devices: 92.8 us -> 0 us
  blocking collectives: 75 us -> 0 us
  Pallas kernels: 0 us -> 62.1 us
  other arithmetic: 52.3 us -> 0.68 us
  matrix products: 17.7 us -> 0 us
  between operations: 13.7 us -> 0.04 us
  starting transfers between devices: 10.1 us -> 0 us
  local copies, waits for them, and re-layouts: 10.1 us -> 3.68 us
    psum x1 -> x0, waiting for transfers between devices: 76.9 us -> none  [local(): lax.psum(factor_table(factor_panel, local_picks, owned_mask), ('rows', 'c...]
    psum x1 -> x0, blocking collectives: 75 us -> none  [local(): lax.psum(pick_table(library, local_picks, owned_mask), ('rows', 'cols', '...]
    pallas_call x0 -> x3, Pallas kernels: none -> 62.1 us  [the longest x1 32.5 us: centered_panels(): pl.pallas_call(panel_kernel, out_shape=jax.ShapeDtypeStruct((BLOCKS, owne...]
    another operation x11 -> x0, other arithmetic: 46.9 us -> none  [the longest x6 24.8 us: local(): cholesky_low = jnp.linalg.cholesky(pivot_block)]
    dot_general x8 -> x0, matrix products: 17.1 us -> none  [the longest x2 8.83 us: local(): jnp.einsum('sf,nf->sn', pick_rows, library, preferred_element_type=jnp.fl...]
    all_to_all x2 -> x0, waiting for transfers between devices: 15.9 us -> none  [regroup(): lax.all_to_all(shaped, ('rows', 'cols', 'sub'), split_axis=0, concat_axis...]
    all_to_all x2 -> x0, starting transfers between devices: 10.1 us -> none  [regroup(): lax.all_to_all(shaped, ('rows', 'cols', 'sub'), split_axis=0, concat_axis...]
    gather x3 -> x0, local copies, waits for them, and re-layouts: 9.06 us -> none  [the longest x2 8.41 us: pick_table(): taken = jnp.take(library, clipped, axis=0).astype(jnp.float32)]
  transfers between devices with their start and end apart: 3 -> 0, of which waited for: 2 -> 0; matrix products, arithmetic and copies ran while one was open for 13% -> 0% of each run, Pallas kernels for 0% -> 0%
where the time goes in v2:
time: 66.6 us; the launch traced here: 66.5 us
  Pallas kernels  62.1 us (93%)
  local copies, waits for them, and re-layouts  3.68 us (6%)
  other arithmetic  0.68 us (1%)
    pallas_call x1, Pallas kernels, centered_panels(): pl.pallas_call(panel_kernel, out_shape=jax.ShapeDtypeStruct((BLOCKS, owne...  32.5 us
    pallas_call x1, Pallas kernels, gather_kernels(): pl.pallas_call(gather_kernel, out_shape=(jax.ShapeDtypeStruct((picks, row...  24.7 us
    pallas_call x1, Pallas kernels, first_inverse(): pl.pallas_call(first_kernel, out_shape=(square,) * 3, in_specs=[vmem], ou...  4.81 us
    unnamed x3, local copies, waits for them, and re-layouts  3.54 us

profile of v2, /device:TPU:0, one launch (start us, length us, event | category | flops | bytes accessed | tf_op | source)
XLA Modules:
  0.0 66.5 jit_solution(711982981439404003)
XLA Ops:
  0.0 0.7 %broadcast_subtract_fusion = s32[256]{0:T(256)S(1)} fusion(s32[256]{0:T(256)} %param.3, s32[]{:T(128)S(6)} %mul.11), kind=kLoop, calls=%fused_computation | loop fusion | flops 256 | bytes 2052 | tf_op jit(solution)/shard_map/sub | solution.py:396
  0.7 0.1 copy.3.local_ref
  0.8 0.0 copy-start
  0.8 2.5 %copy-done = bf16[2560,1024]{1,0:T(8,128)(2,1)S(1)} copy-done((bf16[2560,1024]{1,0:T(8,128)(2,1)S(1)}, bf16[2560,1024]{1,0:T(8,128)(2,1)}, u32[]{:S(2)}) %copy-start) | copy-done | bytes 5242904
  3.3 24.7 %gather_kernels.1 = (f32[256,2560]{1,0:T(8,128)S(1)}, f32[256,256]{1,0:T(8,128)S(1)}) custom-call(s32[256,1]{1,0:T(8,128)S(1)} %copy.3.local_ref, bf16[2560,1024]{1,0:T(8,128)(2,1)S(1)} %copy-done), custom_call_target="tpu_custom_call" | custom-call | tf_op jit(solution)/shard_map/gather_kernels/pallas_call | solution.py:192
  28.0 4.8 %first_inverse.1 = (f32[128,128]{1,0:T(8,128)S(1)}, f32[128,128]{1,0:T(8,128)S(1)}, f32[128,128]{1,0:T(8,128)S(1)}) custom-call(f32[256,256]{1,0:T(8,128)S(1)} %get-tuple-element.10.pivot_ref), custom_call_target="tpu_custom_call" | custom-call | tf_op jit(solution)/shard_map/first_inverse/pallas_call | solution.py:273
  32.8 32.5 %centered_panels.1 = bf16[2,8,40960]{2,1,0:T(8,128)(2,1)S(1)} custom-call(f32[128,128]{1,0:T(8,128)S(1)} %get-tuple-element.11.inverse_ref, f32[128,128]{1,0:T(8,128)S(1)} %get-tuple-element.12.prior_ref, f32[128,128]{1,0:T(8,128)S(1)} %get-tuple-element.13.second_ref, f32[256,2560]{1,0:T(8,128)S(1)} %get-tuple-element.14.kernel_ref), custom_call_target="tpu_custom_call" | custom-call | tf_op jit(solution)/shard_map/centered_panels/pallas_call | solution.py:358
  65.4 1.1 %copy.5 = bf16[2,8,40960]{2,1,0:T(8,128)(2,1)} copy(bf16[2,8,40960]{2,1,0:T(8,128)(2,1)S(1)} %centered_panels.1) | data formatting | bytes 2621440
Async XLA Ops:
  0.8 2.5 %copy-start = (bf16[2560,1024]{1,0:T(8,128)(2,1)S(1)}, bf16[2560,1024]{1,0:T(8,128)(2,1)}, u32[]{:S(2)}) copy-start(bf16[2560,1024]{1,0:T(8,128)(2,1)} %library_ref.1) | copy-start | bytes 15728644

commit v3 on v0

v3 whole, which is shorter than its diff:
```python
import functools

import jax
import jax.numpy as jnp
from jax import lax
from jax.experimental import pallas as pl
from jax.experimental.pallas import tpu as pltpu
from jax.sharding import PartitionSpec as P

BLOCK = 128
BLOCKS = 2
GROUP = 16
SPREAD = ("rows", "cols", "sub")
MESH = pl.DeviceIdType.MESH
HIGHEST = lax.Precision.HIGHEST

nugget = 0.1


def tanimoto(products, left_sq, right_sq):
    return products / (left_sq[:, None] + right_sq[None, :] - products)


def pick_table(library, local_picks, owned_mask):
    clipped = jnp.clip(local_picks, 0, library.shape[0] - 1)
    taken = jnp.take(library, clipped, axis=0).astype(jnp.float32)
    return taken * owned_mask[:, None]


def regroup(block_panel):
    block_count, local_rows = block_panel.shape
    devices_all = lax.axis_size(SPREAD)
    shaped = block_panel.reshape(devices_all, block_count // devices_all, 1, local_rows)
    moved = lax.all_to_all(shaped, SPREAD, split_axis=0, concat_axis=2, tiled=True)
    return moved


def center_rows(moved, owned_count):
    values = moved.reshape(owned_count, -1).astype(jnp.float32)
    column_mean = jnp.mean(values, axis=1, keepdims=True)
    return (values - column_mean).astype(jnp.bfloat16)


def eliminate(left, right, hooks=None):
    size = left.shape[0]
    sub = lax.broadcasted_iota(jnp.int32, (GROUP, size), 0)
    for start in range(0, size, GROUP):
        stop = start + GROUP
        top = left[start:stop, :]
        low = right[start:stop, :]
        columns = [
            jnp.broadcast_to(top[:, start + j : start + j + 1], (GROUP, size)) for j in range(GROUP)
        ]
        pivots = jnp.ones((GROUP, size), jnp.float32)
        for j in range(GROUP):
            pivot = columns[j][j : j + 1, :]
            pivots = jnp.where(sub == j, pivot, pivots)
            factor = jnp.where(sub > j, columns[j] * (1.0 / pivot), 0.0)
            top = top - factor * top[j : j + 1, :]
            low = low - factor * low[j : j + 1, :]
            for k in range(j + 1, GROUP):
                columns[k] = columns[k] - factor * columns[k][j : j + 1, :]
        scale = lax.rsqrt(pivots)
        top = top * scale
        low = low * scale
        right[start:stop, :] = low
        if stop < size:
            side = jnp.transpose(top)[stop:, :]
            both = jnp.concatenate([top, low], axis=1)
            update = jnp.dot(side, both, precision=HIGHEST, preferred_element_type=jnp.float32)
            left[stop:, :] = left[stop:, :] - update[:, :size]
            right[stop:, :] = right[stop:, :] - update[:, size:]
        if hooks and start in hooks:
            hooks[start]()


def identity_of(size):
    ones = lax.broadcasted_iota(jnp.int32, (size, size), 0) == lax.broadcasted_iota(
        jnp.int32, (size, size), 1
    )
    return ones.astype(jnp.float32)


def full_dot(left, right):
    return jnp.dot(left, right, precision=HIGHEST, preferred_element_type=jnp.float32)


def first_kernel(pivot_ref, inverse_ref, prior_ref, second_ref, left):
    left[...] = pivot_ref[:BLOCK, :BLOCK]
    inverse_ref[...] = identity_of(BLOCK)
    eliminate(left, inverse_ref)
    prior = full_dot(inverse_ref[...], pivot_ref[:BLOCK, BLOCK:])
    prior_t = jnp.transpose(prior)
    prior_ref[...] = prior_t
    second_ref[...] = pivot_ref[BLOCK:, BLOCK:] - full_dot(prior_t, prior)


def first_inverse(pivot):
    vmem = pl.BlockSpec(memory_space=pltpu.VMEM)
    square = jax.ShapeDtypeStruct((BLOCK, BLOCK), jnp.float32)
    return pl.pallas_call(
        first_kernel,
        out_shape=(square,) * 3,
        in_specs=[vmem],
        out_specs=(vmem,) * 3,
        scratch_shapes=[pltpu.VMEM((BLOCK, BLOCK), jnp.float32)],
        compiler_params=pltpu.CompilerParams(vmem_limit_bytes=24 * 2**20),
        name="first_inverse",
    )(pivot)


def tile_kernel(products, left_sq, right_sq):
    return products / (left_sq + right_sq - products)


def transposed_dot(left, right):
    return lax.dot_general(
        left, right, (((1,), (1,)), ((), ())), preferred_element_type=jnp.float32
    )


def fused_kernel(
    local_ref, library_ref, out_ref,
    table, picked, near, far, squares, kernel, left, right, panel, sent, landed,
    sub_sem, far_sem, send_sem, recv_sem,
):
    sub = lax.axis_index("sub")
    row, col = lax.axis_index("rows"), lax.axis_index("cols")
    row_count, col_count = lax.axis_size("rows"), lax.axis_size("cols")
    chips = row_count * col_count
    devices = 2 * chips
    chip = row * col_count + col
    me = chip * 2 + sub
    features = table.shape[1]
    rows = library_ref.shape[0]
    half = BLOCK // 2
    owned = BLOCK // devices
    part_rows, part_cols = half // row_count, features // col_count
    other = 1 - sub

    def chip_of(index):
        return {"rows": index // col_count, "cols": lax.rem(index, col_count)}

    def device_of(index):
        return {**chip_of(index // 2), "sub": lax.rem(index, 2)}

    barrier = pltpu.get_barrier_semaphore()
    for k in range(1, devices):
        pl.semaphore_signal(
            barrier, inc=1, device_id=device_of(lax.rem(me + k, devices)), device_id_type=MESH
        )

    def half_rows(block, which):
        return pl.ds(pl.multiple_of(block * BLOCK + which * half, 16), half)

    def part(ref, block, index):
        first = block * BLOCK + sub * half + (index // col_count) * part_rows
        side = lax.rem(index, col_count) * part_cols
        return ref.at[
            pl.ds(pl.multiple_of(first, 16), part_rows),
            pl.ds(pl.multiple_of(side, 128), part_cols),
        ]

    def sub_copy(source, target, slot):
        copy = pltpu.make_async_remote_copy(
            src_ref=source,
            dst_ref=target,
            send_sem=sub_sem.at[0, slot],
            recv_sem=sub_sem.at[1, slot],
            device_id={"sub": other},
            device_id_type=MESH,
        )
        copy.start()
        return copy

    def far_copy(source, target, slot, k):
        copy = pltpu.make_async_remote_copy(
            src_ref=source,
            dst_ref=target,
            send_sem=far_sem.at[0, slot, k - 1],
            recv_sem=far_sem.at[1, slot, k - 1],
            device_id=chip_of(lax.rem(chip + k, chips)),
            device_id_type=MESH,
        )
        copy.start()
        return copy

    chip_order = sorted(range(1, chips), key=lambda k: -min(k, chips - k))
    device_order = sorted(range(1, devices), key=lambda k: -min(k, devices - k))
    flights = {}
    tile = 256

    def block_rows(block):
        return slice(block * BLOCK, (block + 1) * BLOCK)

    def pick_block(block):
        span = block_rows(block)
        hot = local_ref[span, :] == lax.broadcasted_iota(jnp.int32, (BLOCK, rows), 1)
        hot = hot.astype(jnp.float32).astype(jnp.bfloat16)
        for start in range(0, features, tile):
            table[span, start : start + tile] = jnp.dot(
                hot, library_ref[:, start : start + tile], preferred_element_type=jnp.float32
            ).astype(jnp.bfloat16)

    def halve(block):
        flights["halve", block] = sub_copy(
            table.at[half_rows(block, other)], near.at[block], block
        )

    def scatter(block):
        flights["halve", block].wait()
        keep = half_rows(block, sub)
        table[keep, :] = table[keep, :] + near[block]
        flights["scatter", block] = [
            far_copy(
                part(table, block, lax.rem(chip + k, chips)), far.at[block, k - 1], block, k
            )
            for k in chip_order
        ]

    def spread(block):
        for copy in flights["scatter", block]:
            copy.wait()
        total = part(table, block, chip)[...]
        for k in range(1, chips):
            total = total + far[block, k - 1]
        mine = part(picked, block, chip)
        mine[...] = total
        flights["spread", block] = [far_copy(mine, mine, BLOCKS + block, k) for k in chip_order]

    def share(block):
        for copy in flights["spread", block]:
            copy.wait()
        held = picked.at[half_rows(block, sub)]
        flights["share", block] = sub_copy(held, held, BLOCKS + block)

    def square_rows():
        ones = jnp.ones((8, features), jnp.bfloat16)
        for start in range(0, rows, tile):
            values = library_ref[start : start + tile, :].astype(jnp.float32)
            values = values * values
            high = values.astype(jnp.bfloat16)
            low = (values - high.astype(jnp.float32)).astype(jnp.bfloat16)
            squares[:, start : start + tile] = transposed_dot(ones, high) + transposed_dot(
                ones, low
            )

    eye = identity_of(BLOCK)

    def fill(block):
        span = block_rows(block)
        picks = picked[span, :]
        gram = transposed_dot(picks, picks)
        across = jnp.sum(gram * eye, axis=0, keepdims=True)
        down = jnp.sum(gram * eye, axis=1, keepdims=True)
        for start in range(0, rows, tile):
            cols = slice(start, start + tile)
            products = transposed_dot(picks, library_ref[cols, :])
            ids = start + lax.broadcasted_iota(jnp.int32, (BLOCK, tile), 1)
            marker = (local_ref[span, :] == ids).astype(jnp.float32)
            kernel[span, cols] = (
                tile_kernel(products, down, squares[0:1, cols]) + nugget * marker
            )
        return tile_kernel(gram, down, across) + nugget * eye, across, down

    def send_block(block):
        started = []
        for k in device_order:
            peer = lax.rem(me + k, devices)
            copy = pltpu.make_async_remote_copy(
                src_ref=sent.at[block, peer],
                dst_ref=landed.at[block, k - 1],
                send_sem=send_sem.at[block, k - 1],
                recv_sem=recv_sem.at[block, k - 1],
                device_id=device_of(peer),
                device_id_type=MESH,
            )
            copy.start()
            started.append(copy)
        flights["send", block] = started

    wide = 512

    def keep_panel(block, span, values):
        sent[block, :, :, span] = values.reshape(devices, owned, wide).astype(jnp.bfloat16)

    def center(block):
        total = jnp.sum(sent[block, me].astype(jnp.float32), axis=1, keepdims=True)
        for k, copy in zip(device_order, flights["send", block]):
            copy.wait()
            total = total + jnp.sum(
                landed[block, k - 1].astype(jnp.float32), axis=1, keepdims=True
            )
        mean = total / (devices * rows)
        for k in range(devices):
            values = sent[block, me] if k == 0 else landed[block, k - 1]
            source = lax.rem(me + devices - k, devices)
            span = pl.ds(pl.multiple_of(source * rows, 128), rows)
            out_ref[block, :, span] = (values.astype(jnp.float32) - mean).astype(jnp.bfloat16)

    pick_block(0)
    pl.semaphore_wait(barrier, devices - 1)
    halve(0)
    pick_block(1)
    halve(1)
    scatter(0)
    square_rows()
    spread(0)
    share(0)
    scatter(1)
    flights["share", 0].wait()
    pivot, across_0, down_0 = fill(0)
    left[...] = pivot
    right[0] = eye
    eliminate(left, right.at[0], {GROUP: lambda: spread(1), 5 * GROUP: lambda: share(1)})
    for start in range(0, rows, wide):
        span = slice(start, start + wide)
        values = full_dot(right[0], kernel[:BLOCK, span])
        panel[:, span] = values
        keep_panel(0, span, values)
    send_block(0)
    flights["share", 1].wait()
    pivot, across_1, down_1 = fill(1)
    cross = transposed_dot(picked[block_rows(0), :], picked[block_rows(1), :])
    prior = full_dot(right[0], tile_kernel(cross, down_0, across_1))
    prior_t = jnp.transpose(prior)
    left[...] = pivot - full_dot(prior_t, prior)
    right[1] = eye
    eliminate(left, right.at[1])
    for start in range(0, rows, wide):
        span = slice(start, start + wide)
        residual = kernel[BLOCK:, span] - full_dot(prior_t, panel[:, span])
        keep_panel(1, span, full_dot(right[1], residual))
    send_block(1)
    for block in range(BLOCKS):
        center(block)


def fused(library, local_all):
    picks = local_all.shape[0]
    rows, features = library.shape
    row_count, col_count = lax.axis_size("rows"), lax.axis_size("cols")
    chips = row_count * col_count
    devices = 2 * chips
    owned = BLOCK // devices
    half = BLOCK // 2
    vmem = pl.BlockSpec(memory_space=pltpu.VMEM)
    return pl.pallas_call(
        fused_kernel,
        out_shape=jax.ShapeDtypeStruct((BLOCKS, owned, devices * rows), jnp.bfloat16),
        in_specs=[vmem] * 2,
        out_specs=vmem,
        scratch_shapes=[
            pltpu.VMEM((picks, features), jnp.bfloat16),
            pltpu.VMEM((picks, features), jnp.bfloat16),
            pltpu.VMEM((BLOCKS, half, features), jnp.bfloat16),
            pltpu.VMEM(
                (BLOCKS, chips - 1, half // row_count, features // col_count), jnp.bfloat16
            ),
            pltpu.VMEM((8, rows), jnp.float32),
            pltpu.VMEM((picks, rows), jnp.float32),
            pltpu.VMEM((BLOCK, BLOCK), jnp.float32),
            pltpu.VMEM((BLOCKS, BLOCK, BLOCK), jnp.float32),
            pltpu.VMEM((BLOCK, rows), jnp.float32),
            pltpu.VMEM((BLOCKS, devices, owned, rows), jnp.bfloat16),
            pltpu.VMEM((BLOCKS, devices - 1, owned, rows), jnp.bfloat16),
            pltpu.SemaphoreType.DMA((2, 2 * BLOCKS)),
            pltpu.SemaphoreType.DMA((2, 2 * BLOCKS, chips - 1)),
            pltpu.SemaphoreType.DMA((BLOCKS, devices - 1)),
            pltpu.SemaphoreType.DMA((BLOCKS, devices - 1)),
        ],
        compiler_params=pltpu.CompilerParams(
            collective_id=0, has_side_effects=True, vmem_limit_bytes=48 * 2**20
        ),
        name="fused",
    )(local_all[:, None], library)


def whole(pick_rows, library, pick_order, row_ids):
    squares = jnp.sum(jnp.square(library.astype(jnp.float32)), axis=1)
    pick_squares = jnp.sum(jnp.square(pick_rows.astype(jnp.float32)), axis=1)
    pick_products = jnp.dot(pick_rows, pick_rows.T, preferred_element_type=jnp.float32)
    pivot = tanimoto(pick_products, pick_squares, pick_squares)
    pivot = pivot + nugget * jnp.eye(pivot.shape[0], dtype=jnp.float32)
    products = jnp.einsum("sf,nf->sn", pick_rows, library, preferred_element_type=jnp.float32)
    marker = (pick_order[:, None] == row_ids[None, :]).astype(jnp.float32)
    return tanimoto(products, pick_squares, squares) + nugget * marker, pivot


def local(library, pick_order):
    local_rows, features = library.shape
    sizes = {axis: lax.axis_size(axis) for axis in SPREAD}
    devices = lax.axis_size(SPREAD)
    owned_count = BLOCK // devices
    first_row = lax.axis_index(SPREAD) * local_rows
    local_all = pick_order - first_row
    fits = (
        sizes["sub"] == 2
        and BLOCK % (2 * sizes["rows"] * 16) == 0
        and features % (sizes["cols"] * 128) == 0
        and BLOCK % (devices * 8) == 0
        and local_rows % 512 == 0
        and features % 256 == 0
    )
    if fits:
        return fused(library, local_all)
    owned_all = ((local_all >= 0) & (local_all < local_rows)).astype(jnp.float32)
    pick_rows = lax.psum(pick_table(library, local_all, owned_all), SPREAD)
    row_ids = first_row + jnp.arange(local_rows, dtype=jnp.int32)
    kernel, pivot = whole(pick_rows.astype(jnp.bfloat16), library, pick_order, row_ids)
    inverse, prior_rows, second = first_inverse(pivot)
    panel = jnp.dot(inverse, kernel[:BLOCK], precision=HIGHEST)
    moved = regroup(panel.astype(jnp.bfloat16))
    lower = jnp.linalg.cholesky(second)
    identity = jnp.eye(BLOCK, dtype=jnp.float32)
    inverse = lax.linalg.triangular_solve(lower, identity, left_side=True, lower=True)
    residual = kernel[BLOCK:] - jnp.dot(prior_rows, panel, precision=HIGHEST)
    panel = jnp.dot(inverse, residual, precision=HIGHEST)
    results = [center_rows(moved, owned_count)]
    results.append(center_rows(regroup(panel.astype(jnp.bfloat16)), owned_count))
    return jnp.stack(results, axis=0)


def solution(mesh):
    placed = (P(("groups", "rows", "cols", "sub"), None), P("groups"))
    return jax.shard_map(
        local,
        mesh=mesh,
        in_specs=placed,
        out_specs=P("groups", ("rows", "cols", "sub"), None),
        check_vma=False,
    )
```

time: 272 us -> 65.1 us (0.24)
  waiting for transfers between devices: 92.8 us -> 0 us
  blocking collectives: 75 us -> 0 us
  Pallas kernels: 0 us -> 63.1 us
  other arithmetic: 52.3 us -> 0.68 us
  matrix products: 17.7 us -> 0 us
  between operations: 13.7 us -> 0.02 us
  starting transfers between devices: 10.1 us -> 0 us
  local copies, waits for them, and re-layouts: 10.1 us -> 1.19 us
    psum x1 -> x0, waiting for transfers between devices: 76.9 us -> none  [local(): lax.psum(factor_table(factor_panel, local_picks, owned_mask), ('rows', 'c...]
    psum x1 -> x0, blocking collectives: 75 us -> none  [local(): lax.psum(pick_table(library, local_picks, owned_mask), ('rows', 'cols', '...]
    pallas_call x0 -> x1, Pallas kernels: none -> 63.1 us  [fused(): pl.pallas_call(fused_kernel, out_shape=jax.ShapeDtypeStruct((BLOCKS, owne...]
    another operation x11 -> x0, other arithmetic: 46.9 us -> none  [the longest x6 24.8 us: local(): cholesky_low = jnp.linalg.cholesky(pivot_block)]
    dot_general x8 -> x0, matrix products: 17.1 us -> none  [the longest x2 8.83 us: local(): jnp.einsum('sf,nf->sn', pick_rows, library, preferred_element_type=jnp.fl...]
    all_to_all x2 -> x0, waiting for transfers between devices: 15.9 us -> none  [regroup(): lax.all_to_all(shaped, ('rows', 'cols', 'sub'), split_axis=0, concat_axis...]
    all_to_all x2 -> x0, starting transfers between devices: 10.1 us -> none  [regroup(): lax.all_to_all(shaped, ('rows', 'cols', 'sub'), split_axis=0, concat_axis...]
    gather x3 -> x0, local copies, waits for them, and re-layouts: 9.06 us -> none  [the longest x2 8.41 us: pick_table(): taken = jnp.take(library, clipped, axis=0).astype(jnp.float32)]
  transfers between devices with their start and end apart: 3 -> 0, of which waited for: 2 -> 0; matrix products, arithmetic and copies ran while one was open for 13% -> 0% of each run, Pallas kernels for 0% -> 0%
where the time goes in v3:
time: 65.1 us; the launch traced here: 65 us
  Pallas kernels  63.1 us (97%)
  local copies, waits for them, and re-layouts  1.19 us (2%)
  other arithmetic  0.68 us (1%)
    pallas_call x1, Pallas kernels, fused(): pl.pallas_call(fused_kernel, out_shape=jax.ShapeDtypeStruct((BLOCKS, owne...  63.1 us

profile of v3, /device:TPU:0, one launch (start us, length us, event | category | flops | bytes accessed | tf_op | source)
XLA Modules:
  0.0 65.0 jit_solution(16241684343439570243)
XLA Ops:
  0.0 0.7 %broadcast_subtract_fusion = s32[256]{0:T(256)S(1)} fusion(s32[256]{0:T(256)} %param.3, s32[]{:T(128)S(6)} %mul.11), kind=kLoop, calls=%fused_computation | loop fusion | flops 256 | bytes 2052 | tf_op jit(solution)/shard_map/sub | solution.py:396
  0.7 0.1 copy.3.local_ref
  0.8 63.1 %fused.1 = bf16[2,8,40960]{2,1,0:T(8,128)(2,1)S(1)} custom-call(s32[256,1]{1,0:T(8,128)S(1)} %copy.3.local_ref, bf16[2560,1024]{1,0:T(8,128)(2,1)} %library_ref.1), custom_call_target="tpu_custom_call" | custom-call | tf_op jit(solution)/shard_map/fused/pallas_call | solution.py:348
  63.9 1.1 %copy.5 = bf16[2,8,40960]{2,1,0:T(8,128)(2,1)} copy(bf16[2,8,40960]{2,1,0:T(8,128)(2,1)S(1)} %fused.1) | data formatting | bytes 2621440

commit v4 on v3

--- a/solution.py
+++ b/solution.py
@@ -85,6 +85,23 @@
     return jnp.dot(left, right, precision=HIGHEST, preferred_element_type=jnp.float32)
 
 
+def halves(values):
+    high = values.astype(jnp.bfloat16)
+    return high, (values - high.astype(jnp.float32)).astype(jnp.bfloat16)
+
+
+def left_parts(values):
+    high, low = halves(values)
+    return jnp.concatenate([high, low, high], axis=1)
+
+
+def split_dot(parts, right):
+    high, low = halves(right)
+    return jnp.dot(
+        parts, jnp.concatenate([high, high, low], axis=0), preferred_element_type=jnp.float32
+    )
+
+
 def first_kernel(pivot_ref, inverse_ref, prior_ref, second_ref, left):
     left[...] = pivot_ref[:BLOCK, :BLOCK]
     inverse_ref[...] = identity_of(BLOCK)
@@ -235,14 +252,14 @@
         flights["share", block] = sub_copy(held, held, BLOCKS + block)
 
     def square_rows():
-        ones = jnp.ones((8, features), jnp.bfloat16)
         for start in range(0, rows, tile):
             values = library_ref[start : start + tile, :].astype(jnp.float32)
             values = values * values
-            high = values.astype(jnp.bfloat16)
-            low = (values - high.astype(jnp.float32)).astype(jnp.bfloat16)
-            squares[:, start : start + tile] = transposed_dot(ones, high) + transposed_dot(
-                ones, low
+            folded = values[:, :128]
+            for first in range(128, features, 128):
+                folded = folded + values[:, first : first + 128]
+            squares[0:1, start : start + tile] = jnp.sum(
+                jnp.transpose(folded), axis=0, keepdims=True
             )
 
     eye = identity_of(BLOCK)
@@ -312,12 +329,14 @@
     pivot, across_0, down_0 = fill(0)
     left[...] = pivot
     right[0] = eye
-    eliminate(left, right.at[0], {GROUP: lambda: spread(1), 5 * GROUP: lambda: share(1)})
+    eliminate(left, right.at[0], {4 * GROUP: lambda: spread(1)})
+    parts = left_parts(right[0])
     for start in range(0, rows, wide):
         span = slice(start, start + wide)
-        values = full_dot(right[0], kernel[:BLOCK, span])
+        values = split_dot(parts, kernel[:BLOCK, span])
         panel[:, span] = values
         keep_panel(0, span, values)
+    share(1)
     send_block(0)
     flights["share", 1].wait()
     pivot, across_1, down_1 = fill(1)
@@ -327,10 +346,11 @@
     left[...] = pivot - full_dot(prior_t, prior)
     right[1] = eye
     eliminate(left, right.at[1])
+    prior_parts, parts = left_parts(prior_t), left_parts(right[1])
     for start in range(0, rows, wide):
         span = slice(start, start + wide)
-        residual = kernel[BLOCK:, span] - full_dot(prior_t, panel[:, span])
-        keep_panel(1, span, full_dot(right[1], residual))
+        residual = kernel[BLOCK:, span] - split_dot(prior_parts, panel[:, span])
+        keep_panel(1, span, split_dot(parts, residual))
     send_block(1)
     for block in range(BLOCKS):
         center(block)

time: 65.1 us -> 64.1 us (0.985)
  Pallas kernels: 63.1 us -> 62.1 us
    pallas_call x1, Pallas kernels: 63.1 us -> 62.1 us  [fused(): pl.pallas_call(fused_kernel, out_shape=jax.ShapeDtypeStruct((BLOCKS, owne...]
where the time goes in v4:
time: 64.1 us; the launch traced here: 64 us
  Pallas kernels  62.1 us (97%)
  local copies, waits for them, and re-layouts  1.19 us (2%)
  other arithmetic  0.68 us (1%)
    pallas_call x1, Pallas kernels, fused(): pl.pallas_call(fused_kernel, out_shape=jax.ShapeDtypeStruct((BLOCKS, owne...  62.1 us

profile of v4, /device:TPU:0, one launch (start us, length us, event | category | flops | bytes accessed | tf_op | source)
XLA Modules:
  0.0 64.0 jit_solution(17979807228019243782)
XLA Ops:
  0.0 0.7 %broadcast_subtract_fusion = s32[256]{0:T(256)S(1)} fusion(s32[256]{0:T(256)} %param.3, s32[]{:T(128)S(6)} %mul.11), kind=kLoop, calls=%fused_computation | loop fusion | flops 256 | bytes 2052 | tf_op jit(solution)/shard_map/sub | solution.py:416
  0.7 0.1 copy.3.local_ref
  0.8 62.1 %fused.1 = bf16[2,8,40960]{2,1,0:T(8,128)(2,1)S(1)} custom-call(s32[256,1]{1,0:T(8,128)S(1)} %copy.3.local_ref, bf16[2560,1024]{1,0:T(8,128)(2,1)} %library_ref.1), custom_call_target="tpu_custom_call" | custom-call | tf_op jit(solution)/shard_map/fused/pallas_call | solution.py:368
  62.9 1.1 %copy.5 = bf16[2,8,40960]{2,1,0:T(8,128)(2,1)} copy(bf16[2,8,40960]{2,1,0:T(8,128)(2,1)S(1)} %fused.1) | data formatting | bytes 2621440

commit v5 on v4

--- a/solution.py
+++ b/solution.py
@@ -319,8 +319,8 @@
     pl.semaphore_wait(barrier, devices - 1)
     halve(0)
     pick_block(1)
+    scatter(0)
     halve(1)
-    scatter(0)
     square_rows()
     spread(0)
     share(0)
@@ -329,7 +329,7 @@
     pivot, across_0, down_0 = fill(0)
     left[...] = pivot
     right[0] = eye
-    eliminate(left, right.at[0], {4 * GROUP: lambda: spread(1)})
+    eliminate(left, right.at[0], {2 * GROUP: lambda: spread(1)})
     parts = left_parts(right[0])
     for start in range(0, rows, wide):
         span = slice(start, start + wide)

time: 64.1 us -> 64.1 us (level)
  no operation moved by 1% of the time
where the time goes in v5:
time: 64.1 us; the launch traced here: 63.9 us
  Pallas kernels  62 us (97%)
  local copies, waits for them, and re-layouts  1.19 us (2%)
  other arithmetic  0.68 us (1%)
    pallas_call x1, Pallas kernels, fused(): pl.pallas_call(fused_kernel, out_shape=jax.ShapeDtypeStruct((BLOCKS, owne...  62 us

profile of v5, /device:TPU:0, one launch (start us, length us, event | category | flops | bytes accessed | tf_op | source)
XLA Modules:
  0.0 63.9 jit_solution(4002001243853790556)
XLA Ops:
  0.0 0.7 %broadcast_subtract_fusion = s32[256]{0:T(256)S(1)} fusion(s32[256]{0:T(256)} %param.3, s32[]{:T(128)S(6)} %mul.11), kind=kLoop, calls=%fused_computation | loop fusion | flops 256 | bytes 2052 | tf_op jit(solution)/shard_map/sub | solution.py:416
  0.7 0.1 copy.3.local_ref
  0.8 62.0 %fused.1 = bf16[2,8,40960]{2,1,0:T(8,128)(2,1)S(1)} custom-call(s32[256,1]{1,0:T(8,128)S(1)} %copy.3.local_ref, bf16[2560,1024]{1,0:T(8,128)(2,1)} %library_ref.1), custom_call_target="tpu_custom_call" | custom-call | tf_op jit(solution)/shard_map/fused/pallas_call | solution.py:368
  62.9 1.1 %copy.5 = bf16[2,8,40960]{2,1,0:T(8,128)(2,1)} copy(bf16[2,8,40960]{2,1,0:T(8,128)(2,1)S(1)} %fused.1) | data formatting | bytes 2621440
